TPU v7x, 32 devices: a whole 2x2x4 slice. The times are simulated.
32 devices in a mesh: row: 8 (over y, x, core), col: 4 (over z).
Axes of the slice: x: 2, y: 2, z: 4, core: 2. Of those that a mesh axis runs over, the one named last changes fastest.
Arguments:
- sensitivity: float32 [16384, 16384], P('row', 'col'), as said below
- injection: float32 [16384, 1024], P('col', 'row'), may hold values from -6 to 6
- dispatch_now: float32 [16384, 1024], P('row', 'col'), may hold values from -3 to 3
- limit_class: int32 [16384], P('row'), may hold values from 0 to 15
- box_table: float32 [16], replicated, may hold values from 0.3 to 1.5
- owner_index: int32 [16384, 1], P('row'), may hold values from 0 to 7; in each aligned block of 2048 rows (0 to 2047, 2048 to 4095, ...) at most 768 rows name the same one
- member_slot: int32 [16384], P('row'), may hold values from 0 to 127
- agg_limit: float32 [1024], P('row'), may hold values from 0.5 to 4
Outputs:
- dispatch: float32 [16384, 1024], P('row', 'col')
- aggregate: float32 [1024, 1024], P('row', 'col')
Inputs may be any that keep to these rules, and one draw needn't show every extreme that they name: `sensitivity`: symmetric. `owner_index`: in each aligned block of 2048 inverters (those of one index of row) at most 768 have the same owner, and some owner has exactly 768 in some block.
All inputs are finite; a program needn't handle non-finite values.
Results may differ from a plain program's by a relative error of at most 0.000088.
Values sent between devices are 32-bit elements; how exact they have to be, the bound alone decides.
A program may use at most 128 MiB of HBM per device.

v0:
```python
import jax
import jax.numpy as jnp
from jax import lax
from jax.sharding import PartitionSpec as P

step_size = 0.1
chunks = 4


def rounded(x):
    return lax.reduce_precision(x, exponent_bits=8, mantissa_bits=7)


def split3(x):
    hi = rounded(x)
    rest = x - hi
    mid = rounded(rest)
    return tuple((part.astype(jnp.bfloat16) for part in (hi, mid, rest - mid)))


def body(
    sensitivity,
    injection,
    dispatch_now,
    limit_class,
    box_table,
    owner_index,
    member_slot,
    agg_limit,
):
    owners = lax.axis_size("row")
    agg_dev = agg_limit.shape[0]
    row_count = sensitivity.shape[0]
    injection_t = injection.T
    width = injection_t.shape[0] // chunks
    group = owners // lax.axis_size("col")
    gradients = []
    for chunk in range(chunks):
        part = injection_t[chunk * width : (chunk + 1) * width]
        part = lax.all_gather(part, "row", axis=0, tiled=True)
        partial_value = lax.dot_general(
            part,
            sensitivity,
            (((1,), (1,)), ((), ())),
            precision=lax.Precision.HIGH,
            preferred_element_type=jnp.float32,
        )
        summed = lax.psum_scatter(partial_value, "col", scatter_dimension=0, tiled=True)
        gradients.append(summed.reshape(group, width, row_count))
    gradient = 2.0 * jnp.concatenate(gradients, axis=1).reshape(-1, row_count).T
    classes = jnp.arange(box_table.shape[0], dtype=jnp.int32)
    box_bound = jnp.sum(
        jnp.where(limit_class[:, None] == classes[None, :], box_table[None, :], 0.0), axis=1
    )[:, None]
    stepped = jnp.clip(dispatch_now - step_size * gradient, -box_bound, box_bound)
    agg_id = owner_index[:, 0] * agg_dev + member_slot
    aggs = owners * agg_dev
    selector = (agg_id[None, :] == jnp.arange(aggs, dtype=jnp.int32)[:, None]).astype(jnp.bfloat16)

    def pick(left, parts, dims):
        return sum(
            (
                lax.dot_general(left, part, (dims, ((), ())), preferred_element_type=jnp.float32)
                for part in parts
            )
        )

    local = pick(selector, split3(stepped), ((1,), (0,)))
    total = lax.psum_scatter(local, "row", scatter_dimension=0, tiled=True)
    limit_col = agg_limit[:, None]
    factor = limit_col / jnp.maximum(jnp.abs(total), limit_col)
    aggregate = total * factor
    all_factor = lax.all_gather(factor, "row", axis=0, tiled=True)
    own_factor = pick(selector, split3(all_factor), ((0,), (0,)))
    return (stepped * own_factor, aggregate)


def solution(mesh):
    placed = (
        P("row", "col"),
        P("col", "row"),
        P("row", "col"),
        P("row"),
        P(),
        P("row", None),
        P("row"),
        P("row"),
    )
    return jax.shard_map(
        body,
        mesh=mesh,
        in_specs=placed,
        out_specs=(P("row", "col"), P("row", "col")),
        check_vma=False,
    )
```

profile of v0, /device:TPU:0, one launch (start us, length us, event | category | flops | bytes accessed | tf_op | source)
XLA Modules:
  0.0 439.6 jit_solution(8798306970045158717)
XLA Ops:
  7.2 1.9 copy.13
  9.1 1.4 fusion.24
  10.6 0.7 all-gather.8.cloned.1.call-update
  11.3 0.7 all-gather.10.cloned.1.call-update
  12.1 0.5 all-gather.12.cloned.1.call-update
  12.6 37.5 %all-gather.6.cloned.1.call-done = f32[256,4096]{1,0:T(8,128)} async-done(((f32[32,4096]{1,0:T(8,128)}), f32[256,4096]{1,0:T(8,128)}) %all-gather.6.cloned.1.call-update) | async-done | bytes 4194320 | tf_op jit(solution)/shard_map/all_gather | solution.py:40
  50.1 20.0 %fusion.25 = f32[256,2048]{1,0:T(8,128)} fusion(f32[256,4096]{1,0:T(8,128)} %all-gather.6.cloned.1.call-done, f32[2048,4096]{1,0:T(8,128)} %param.8), kind=kOutput, calls=%fused_computation.38 | convolution fusion | flops 12884901888 | bytes 39845888 | tf_op jit(solution)/shard_map/dot_general | solution.py:41
  70.2 18.6 %all-gather.8.cloned.1.call-done = f32[256,4096]{1,0:T(8,128)} async-done(((f32[32,4096]{1,0:T(8,128)}), f32[256,4096]{1,0:T(8,128)}) %all-gather.8.cloned.1.call-update) | async-done | bytes 4194320 | tf_op jit(solution)/shard_map/all_gather | solution.py:40
  88.8 20.0 %fusion.26 = f32[256,2048]{1,0:T(8,128)} fusion(f32[256,4096]{1,0:T(8,128)} %all-gather.8.cloned.1.call-done, f32[2048,4096]{1,0:T(8,128)} %param.8), kind=kOutput, calls=%fused_computation.39 | convolution fusion | flops 12884901888 | bytes 39845888 | tf_op jit(solution)/shard_map/dot_general | solution.py:41
  109.1 18.4 %all-gather.10.cloned.1.call-done = f32[256,4096]{1,0:T(8,128)} async-done(((f32[32,4096]{1,0:T(8,128)}), f32[256,4096]{1,0:T(8,128)}) %all-gather.10.cloned.1.call-update) | async-done | bytes 4194320 | tf_op jit(solution)/shard_map/all_gather | solution.py:40
  127.5 20.0 %fusion.27 = f32[256,2048]{1,0:T(8,128)} fusion(f32[256,4096]{1,0:T(8,128)} %all-gather.10.cloned.1.call-done, f32[2048,4096]{1,0:T(8,128)} %param.8), kind=kOutput, calls=%fused_computation.40 | convolution fusion | flops 12884901888 | bytes 39845888 | tf_op jit(solution)/shard_map/dot_general | solution.py:41
  147.5 18.4 %all-gather.12.cloned.1.call-done = f32[256,4096]{1,0:T(8,128)} async-done(((f32[32,4096]{1,0:T(8,128)}), f32[256,4096]{1,0:T(8,128)}) %all-gather.12.cloned.1.call-update) | async-done | bytes 4194320 | tf_op jit(solution)/shard_map/all_gather | solution.py:40
  166.0 19.8 %fusion.28 = f32[256,2048]{1,0:T(8,128)} fusion(f32[256,4096]{1,0:T(8,128)} %all-gather.12.cloned.1.call-done, f32[2048,4096]{1,0:T(8,128)} %param.8), kind=kOutput, calls=%fused_computation.41 | convolution fusion | flops 12884901888 | bytes 39845888 | tf_op jit(solution)/shard_map/dot_general | solution.py:41
  185.8 0.3 reduce-scatter.14.cloned.1.call-start
  186.1 0.4 copy-done.3
  186.7 25.3 %reduce-scatter.6.cloned.1.call-done = f32[64,2048]{1,0:T(8,128)} async-done(((f32[256,2048]{1,0:T(8,128)}), f32[64,2048]{1,0:T(8,128)}) %reduce-scatter.6.cloned.1.call-update) | async-done | bytes 524304 | tf_op jit(solution)/shard_map/reduce_scatter | solution.py:48
  212.0 45.5 %reduce-scatter.8.cloned.1.call-done = f32[64,2048]{1,0:T(8,128)} async-done(((f32[256,2048]{1,0:T(8,128)}), f32[64,2048]{1,0:T(8,128)}) %reduce-scatter.8.cloned.1.call-update) | async-done | bytes 524304 | tf_op jit(solution)/shard_map/reduce_scatter | solution.py:48
  257.5 45.5 %reduce-scatter.10.cloned.1.call-done = f32[64,2048]{1,0:T(8,128)} async-done(((f32[256,2048]{1,0:T(8,128)}), f32[64,2048]{1,0:T(8,128)}) %reduce-scatter.10.cloned.1.call-update) | async-done | bytes 524304 | tf_op jit(solution)/shard_map/reduce_scatter | solution.py:48
  303.0 46.2 %reduce-scatter.12.cloned.1.call-done = f32[64,2048]{1,0:T(8,128)} async-done(((f32[256,2048]{1,0:T(8,128)}), f32[64,2048]{1,0:T(8,128)}) %reduce-scatter.12.cloned.1.call-update) | async-done | bytes 524304 | tf_op jit(solution)/shard_map/reduce_scatter | solution.py:48
  349.2 3.1 maximum_multiply_fusion
  352.3 1.9 copy.15
  354.2 1.9 fusion.17
  356.2 1.7 fusion.3
  357.9 1.6 fusion.4
  359.5 2.5 fusion.19
  362.0 0.3 all-gather.14.cloned.1.call-start
  362.4 35.2 %reduce-scatter.14.cloned.1.call-done = f32[128,256]{1,0:T(8,128)} async-done(((f32[1024,256]{1,0:T(8,128)}), f32[128,256]{1,0:T(8,128)}) %reduce-scatter.14.cloned.1.call-update) | async-done | bytes 131088 | tf_op jit(solution)/shard_map/reduce_scatter | solution.py:69
  397.6 1.7 fusion.23
  399.3 23.6 %all-gather.14.cloned.1.call-done = f32[1024,256]{1,0:T(8,128)} async-done(((f32[128,256]{1,0:T(8,128)}), f32[1024,256]{1,0:T(8,128)}) %all-gather.14.cloned.1.call-update) | async-done | bytes 1048592 | tf_op jit(solution)/shard_map/all_gather | solution.py:73
  422.9 3.7 fusion.1
  426.6 2.4 fusion.12
  429.1 3.7 fusion.14
  (34 shorter events, 0.8 us)
Async XLA Ops:
  7.2 42.9 %all-gather.6.cloned.1.call-start = ((), (), s32[]{:S(2)}) async-start(), calls=%async_computation.5 | async-start | bytes 4718592 | tf_op jit(solution)/shard_map/all_gather | solution.py:40
  10.5 78.3 %all-gather.8.cloned.1.call-start = ((), (), s32[]{:S(2)}) async-start(), calls=%async_computation.7 | async-start | bytes 4718592 | tf_op jit(solution)/shard_map/all_gather | solution.py:40
  11.3 116.2 %all-gather.10.cloned.1.call-start = ((), (), s32[]{:S(2)}) async-start(), calls=%async_computation.9 | async-start | bytes 4718592 | tf_op jit(solution)/shard_map/all_gather | solution.py:40
  12.0 154.0 %all-gather.12.cloned.1.call-start = ((), (), s32[]{:S(2)}) async-start(), calls=%async_computation.11 | async-start | bytes 4718592 | tf_op jit(solution)/shard_map/all_gather | solution.py:40
  12.6 199.4 %reduce-scatter.6.cloned.1.call-start = ((), (), s32[]{:S(2)}) async-start(), calls=%async_computation.6 | async-start | bytes 2621440 | tf_op jit(solution)/shard_map/reduce_scatter | solution.py:48
  70.2 187.3 %reduce-scatter.8.cloned.1.call-start = ((), (), s32[]{:S(2)}) async-start(), calls=%async_computation.8 | async-start | bytes 2621440 | tf_op jit(solution)/shard_map/reduce_scatter | solution.py:48
  108.9 194.1 %reduce-scatter.10.cloned.1.call-start = ((), (), s32[]{:S(2)}) async-start(), calls=%async_computation.10 | async-start | bytes 2621440 | tf_op jit(solution)/shard_map/reduce_scatter | solution.py:48
  147.5 201.7 %reduce-scatter.12.cloned.1.call-start = ((), (), s32[]{:S(2)}) async-start(), calls=%async_computation.12 | async-start | bytes 2621440 | tf_op jit(solution)/shard_map/reduce_scatter | solution.py:48
  185.8 0.7 copy-start.3
  185.8 0.7 copy-start.6
  185.8 0.8 copy-start.4
  185.8 0.8 copy-start.2
  185.8 211.7 %reduce-scatter.14.cloned.1.call-start = ((), (), s32[]{:S(2)}) async-start(), calls=%async_computation.13 | async-start | bytes 1179648 | tf_op jit(solution)/shard_map/reduce_scatter | solution.py:69
  356.2 3.3 copy-start
  359.5 38.1 %copy-start.5 = (f32[128]{0:T(128)S(1)}, f32[128]{0:T(128)}, u32[]{:S(2)}) copy-start(f32[128]{0:T(128)} %param.15) | copy-start | bytes 1540
  362.0 60.8 %all-gather.14.cloned.1.call-start = ((), (), s32[]{:S(2)}) async-start(), calls=%async_computation.14 | async-start | bytes 1179648 | tf_op jit(solution)/shard_map/all_gather | solution.py:73
  422.9 3.7 copy-start.7
  426.6 2.4 copy-start.1
Sparse Core Ops, SparseCore 0:
  10.6 39.4 all-gather.5
  52.0 36.7 all-gather.7
  90.7 36.7 all-gather.9
  129.2 36.7 all-gather.11
  168.1 43.8 reduce-scatter.5
  214.2 43.1 reduce-scatter.7
  259.8 43.1 reduce-scatter.9
  305.9 43.1 reduce-scatter.11
  362.2 35.3 reduce-scatter.13
  399.4 23.4 all-gather.13
where the time goes:
time: 440 us
  waiting for transfers between devices  316 us (72%)
  matrix products  95.5 us (22%)
  between operations  14.3 us (3%)
  other arithmetic  6.87 us (2%)
  local copies, waits for them, and re-layouts  5.62 us (1%)
    reduce_scatter x4, waiting for transfers between devices, body(): lax.psum_scatter(partial_value, 'col', scatter_dimension=0, tiled=True)  162 us
    all_gather x4, waiting for transfers between devices, body(): part = lax.all_gather(part, 'row', axis=0, tiled=True)  92.9 us
    dot_general x4, matrix products, body(): lax.dot_general(part, sensitivity, (((1,), (1,)), ((), ())), precision=la...  79.9 us
    reduce_scatter x1, waiting for transfers between devices, body(): total = lax.psum_scatter(local, 'row', scatter_dimension=0, tiled=True)  35.2 us
    all_gather x1, waiting for transfers between devices, body(): all_factor = lax.all_gather(factor, 'row', axis=0, tiled=True)  23.6 us
    dot_general x6, matrix products, pick(): lax.dot_general(left, part, (dims, ((), ())), preferred_element_type=jnp....  15.6 us
  transfers between devices with their start and end apart: 10, of which 10 were waited for; matrix products, arithmetic and copies ran while one was open for 18% of the time, Pallas kernels for 0%

commit v1 on v0

--- a/solution.py
+++ b/solution.py
@@ -70,7 +70,12 @@
     limit_col = agg_limit[:, None]
     factor = limit_col / jnp.maximum(jnp.abs(total), limit_col)
     aggregate = total * factor
-    all_factor = lax.all_gather(factor, "row", axis=0, tiled=True)
+    ring = [factor]
+    for hop in range(7):
+        ring.append(lax.ppermute(ring[-1], "row", [(dev, (dev + 1) % 8) for dev in range(8)]))
+    all_factor = jnp.roll(
+        jnp.concatenate(ring[::-1], axis=0), (lax.axis_index("row") + 1) * ring[0].shape[0], axis=0
+    )
     own_factor = pick(selector, split3(all_factor), ((0,), (0,)))
     return (stepped * own_factor, aggregate)
 

time: 440 us -> 452 us (1.027)
  waiting for transfers between devices: 316 us -> 330 us
    ppermute x0 -> x7, waiting for transfers between devices: none -> 37 us  [body(): lax.ppermute(ring[-1], 'row', [(dev, (dev + 1) % 8) for dev in range(8)])]
    all_gather x1 -> x0, waiting for transfers between devices: 23.6 us -> none  [body(): all_factor = lax.all_gather(factor, 'row', axis=0, tiled=True)]
  transfers between devices with their start and end apart: 10 -> 16, of which waited for: 10 -> 16; matrix products, arithmetic and copies ran while one was open for 18% -> 18% of each run, Pallas kernels for 0% -> 0%
where the time goes in v1:
time: 452 us
  waiting for transfers between devices  330 us (73%)
  matrix products  94.2 us (21%)
  between operations  14.1 us (3%)
  other arithmetic  7.09 us (2%)
  local copies, waits for them, and re-layouts  5.76 us (1%)
    reduce_scatter x4, waiting for transfers between devices, body(): lax.psum_scatter(partial_value, 'col', scatter_dimension=0, tiled=True)  162 us
    all_gather x4, waiting for transfers between devices, body(): part = lax.all_gather(part, 'row', axis=0, tiled=True)  92.9 us
    dot_general x4, matrix products, body(): lax.dot_general(part, sensitivity, (((1,), (1,)), ((), ())), precision=la...  79.9 us
    ppermute x7, waiting for transfers between devices, body(): lax.ppermute(ring[-1], 'row', [(dev, (dev + 1) % 8) for dev in range(8)])  37 us
    reduce_scatter x1, waiting for transfers between devices, body(): total = lax.psum_scatter(local, 'row', scatter_dimension=0, tiled=True)  35.5 us
    dot_general x6, matrix products, pick(): lax.dot_general(left, part, (dims, ((), ())), preferred_element_type=jnp....  14.4 us
  transfers between devices with their start and end apart: 16, of which 16 were waited for; matrix products, arithmetic and copies ran while one was open for 18% of the time, Pallas kernels for 0%

profile of v1, /device:TPU:0, one launch (start us, length us, event | category | flops | bytes accessed | tf_op | source)
XLA Modules:
  0.0 452.0 jit_solution(11374321473594309868)
XLA Ops:
  7.2 1.9 copy.13
  9.1 1.3 fusion.27
  12.6 37.5 %all-gather.5.cloned.1.call-done = f32[256,4096]{1,0:T(8,128)} async-done(((f32[32,4096]{1,0:T(8,128)}), f32[256,4096]{1,0:T(8,128)}) %all-gather.5.cloned.1.call-update) | async-done | bytes 4194320 | tf_op jit(solution)/shard_map/all_gather | solution.py:40
  50.1 20.0 %fusion.28 = f32[256,2048]{1,0:T(8,128)} fusion(f32[256,4096]{1,0:T(8,128)} %all-gather.5.cloned.1.call-done, f32[2048,4096]{1,0:T(8,128)} %param.8), kind=kOutput, calls=%fused_computation.57 | convolution fusion | flops 12884901888 | bytes 39845888 | tf_op jit(solution)/shard_map/dot_general | solution.py:41
  70.2 18.6 %all-gather.7.cloned.1.call-done = f32[256,4096]{1,0:T(8,128)} async-done(((f32[32,4096]{1,0:T(8,128)}), f32[256,4096]{1,0:T(8,128)}) %all-gather.7.cloned.1.call-update) | async-done | bytes 4194320 | tf_op jit(solution)/shard_map/all_gather | solution.py:40
  88.8 20.0 %fusion.29 = f32[256,2048]{1,0:T(8,128)} fusion(f32[256,4096]{1,0:T(8,128)} %all-gather.7.cloned.1.call-done, f32[2048,4096]{1,0:T(8,128)} %param.8), kind=kOutput, calls=%fused_computation.58 | convolution fusion | flops 12884901888 | bytes 39845888 | tf_op jit(solution)/shard_map/dot_general | solution.py:41
  109.1 18.4 %all-gather.9.cloned.1.call-done = f32[256,4096]{1,0:T(8,128)} async-done(((f32[32,4096]{1,0:T(8,128)}), f32[256,4096]{1,0:T(8,128)}) %all-gather.9.cloned.1.call-update) | async-done | bytes 4194320 | tf_op jit(solution)/shard_map/all_gather | solution.py:40
  127.5 20.0 %fusion.30 = f32[256,2048]{1,0:T(8,128)} fusion(f32[256,4096]{1,0:T(8,128)} %all-gather.9.cloned.1.call-done, f32[2048,4096]{1,0:T(8,128)} %param.8), kind=kOutput, calls=%fused_computation.59 | convolution fusion | flops 12884901888 | bytes 39845888 | tf_op jit(solution)/shard_map/dot_general | solution.py:41
  147.5 18.4 %all-gather.11.cloned.1.call-done = f32[256,4096]{1,0:T(8,128)} async-done(((f32[32,4096]{1,0:T(8,128)}), f32[256,4096]{1,0:T(8,128)}) %all-gather.11.cloned.1.call-update) | async-done | bytes 4194320 | tf_op jit(solution)/shard_map/all_gather | solution.py:40
  165.9 19.8 %fusion.31 = f32[256,2048]{1,0:T(8,128)} fusion(f32[256,4096]{1,0:T(8,128)} %all-gather.11.cloned.1.call-done, f32[2048,4096]{1,0:T(8,128)} %param.8), kind=kOutput, calls=%fused_computation.60 | convolution fusion | flops 12884901888 | bytes 39845888 | tf_op jit(solution)/shard_map/dot_general | solution.py:41
  186.6 25.3 %reduce-scatter.6.cloned.1.call-done = f32[64,2048]{1,0:T(8,128)} async-done(((f32[256,2048]{1,0:T(8,128)}), f32[64,2048]{1,0:T(8,128)}) %reduce-scatter.6.cloned.1.call-update) | async-done | bytes 524304 | tf_op jit(solution)/shard_map/reduce_scatter | solution.py:48
  212.0 45.5 %reduce-scatter.8.cloned.1.call-done = f32[64,2048]{1,0:T(8,128)} async-done(((f32[256,2048]{1,0:T(8,128)}), f32[64,2048]{1,0:T(8,128)}) %reduce-scatter.8.cloned.1.call-update) | async-done | bytes 524304 | tf_op jit(solution)/shard_map/reduce_scatter | solution.py:48
  257.5 45.5 %reduce-scatter.10.cloned.1.call-done = f32[64,2048]{1,0:T(8,128)} async-done(((f32[256,2048]{1,0:T(8,128)}), f32[64,2048]{1,0:T(8,128)}) %reduce-scatter.10.cloned.1.call-update) | async-done | bytes 524304 | tf_op jit(solution)/shard_map/reduce_scatter | solution.py:48
  303.0 46.2 %reduce-scatter.12.cloned.1.call-done = f32[64,2048]{1,0:T(8,128)} async-done(((f32[256,2048]{1,0:T(8,128)}), f32[64,2048]{1,0:T(8,128)}) %reduce-scatter.12.cloned.1.call-update) | async-done | bytes 524304 | tf_op jit(solution)/shard_map/reduce_scatter | solution.py:48
  349.1 3.1 maximum_multiply_fusion
  352.3 1.9 copy.15
  354.2 1.9 fusion.17
  356.2 1.7 fusion.3
  357.9 1.6 fusion.4
  359.5 2.6 fusion.19
  362.0 35.5 %reduce-scatter.14.cloned.1.call-done = f32[128,256]{1,0:T(8,128)} async-done(((f32[1024,256]{1,0:T(8,128)}), f32[128,256]{1,0:T(8,128)}) %reduce-scatter.14.cloned.1.call-update) | async-done | bytes 131088 | tf_op jit(solution)/shard_map/reduce_scatter | solution.py:69
  397.6 1.1 maximum_divide_fusion
  398.7 5.3 %collective-permute-done = f32[128,256]{1,0:T(8,128)S(1)} collective-permute-done((f32[128,256]{1,0:T(8,128)S(1)}, f32[128,256]{1,0:T(8,128)S(1)}, u32[]{:S(2)}, u32[]{:S(2)}) %collective-permute-start) | collective-permute-done | bytes 131104 | tf_op jit(solution)/shard_map/ppermute | solution.py:75
  404.0 5.3 %collective-permute-done.1 = f32[128,256]{1,0:T(8,128)S(1)} collective-permute-done((f32[128,256]{1,0:T(8,128)S(1)}, f32[128,256]{1,0:T(8,128)S(1)}, u32[]{:S(2)}, u32[]{:S(2)}) %collective-permute-start.1) | collective-permute-done | bytes 131104 | tf_op jit(solution)/shard_map/ppermute | solution.py:75
  409.3 5.3 %collective-permute-done.2 = f32[128,256]{1,0:T(8,128)S(1)} collective-permute-done((f32[128,256]{1,0:T(8,128)S(1)}, f32[128,256]{1,0:T(8,128)S(1)}, u32[]{:S(2)}, u32[]{:S(2)}) %collective-permute-start.2) | collective-permute-done | bytes 131104 | tf_op jit(solution)/shard_map/ppermute | solution.py:75
  414.6 5.3 %collective-permute-done.3 = f32[128,256]{1,0:T(8,128)S(1)} collective-permute-done((f32[128,256]{1,0:T(8,128)S(1)}, f32[128,256]{1,0:T(8,128)S(1)}, u32[]{:S(2)}, u32[]{:S(2)}) %collective-permute-start.3) | collective-permute-done | bytes 131104 | tf_op jit(solution)/shard_map/ppermute | solution.py:75
  419.9 5.3 %collective-permute-done.4 = f32[128,256]{1,0:T(8,128)S(1)} collective-permute-done((f32[128,256]{1,0:T(8,128)S(1)}, f32[128,256]{1,0:T(8,128)S(1)}, u32[]{:S(2)}, u32[]{:S(2)}) %collective-permute-start.4) | collective-permute-done | bytes 131104 | tf_op jit(solution)/shard_map/ppermute | solution.py:75
  425.1 5.3 %collective-permute-done.5 = f32[128,256]{1,0:T(8,128)S(1)} collective-permute-done((f32[128,256]{1,0:T(8,128)S(1)}, f32[128,256]{1,0:T(8,128)S(1)}, u32[]{:S(2)}, u32[]{:S(2)}) %collective-permute-start.5) | collective-permute-done | bytes 131104 | tf_op jit(solution)/shard_map/ppermute | solution.py:75
  430.4 5.3 %collective-permute-done.6 = f32[128,256]{1,0:T(8,128)S(1)} collective-permute-done((f32[128,256]{1,0:T(8,128)S(1)}, f32[128,256]{1,0:T(8,128)S(1)}, u32[]{:S(2)}, u32[]{:S(2)}) %collective-permute-start.6) | collective-permute-done | bytes 131104 | tf_op jit(solution)/shard_map/ppermute | solution.py:75
  436.9 2.4 fusion.1
  439.3 2.4 fusion.12
  441.7 3.7 fusion.14
  (61 shorter events, 4.4 us)
Async XLA Ops:
  7.2 42.9 %all-gather.5.cloned.1.call-start = ((), (), s32[]{:S(2)}) async-start(), calls=%async_computation.5 | async-start | bytes 4718592 | tf_op jit(solution)/shard_map/all_gather | solution.py:40
  10.5 78.3 %all-gather.7.cloned.1.call-start = ((), (), s32[]{:S(2)}) async-start(), calls=%async_computation.7 | async-start | bytes 4718592 | tf_op jit(solution)/shard_map/all_gather | solution.py:40
  11.3 116.2 %all-gather.9.cloned.1.call-start = ((), (), s32[]{:S(2)}) async-start(), calls=%async_computation.9 | async-start | bytes 4718592 | tf_op jit(solution)/shard_map/all_gather | solution.py:40
  12.0 154.0 %all-gather.11.cloned.1.call-start = ((), (), s32[]{:S(2)}) async-start(), calls=%async_computation.11 | async-start | bytes 4718592 | tf_op jit(solution)/shard_map/all_gather | solution.py:40
  12.6 199.4 %reduce-scatter.6.cloned.1.call-start = ((), (), s32[]{:S(2)}) async-start(), calls=%async_computation.6 | async-start | bytes 2621440 | tf_op jit(solution)/shard_map/reduce_scatter | solution.py:48
  70.1 187.3 %reduce-scatter.8.cloned.1.call-start = ((), (), s32[]{:S(2)}) async-start(), calls=%async_computation.8 | async-start | bytes 2621440 | tf_op jit(solution)/shard_map/reduce_scatter | solution.py:48
  108.8 194.1 %reduce-scatter.10.cloned.1.call-start = ((), (), s32[]{:S(2)}) async-start(), calls=%async_computation.10 | async-start | bytes 2621440 | tf_op jit(solution)/shard_map/reduce_scatter | solution.py:48
  147.5 201.7 %reduce-scatter.12.cloned.1.call-start = ((), (), s32[]{:S(2)}) async-start(), calls=%async_computation.12 | async-start | bytes 2621440 | tf_op jit(solution)/shard_map/reduce_scatter | solution.py:48
  185.8 0.7 copy-start.4
  185.8 0.7 copy-start.7
  185.8 0.8 copy-start.5
  185.8 0.8 copy-start.3
  185.8 211.7 %reduce-scatter.14.cloned.1.call-start = ((), (), s32[]{:S(2)}) async-start(), calls=%async_computation.13 | async-start | bytes 1179648 | tf_op jit(solution)/shard_map/reduce_scatter | solution.py:69
  356.1 3.3 copy-start
  359.5 38.1 %copy-start.6 = (f32[128]{0:T(128)S(1)}, f32[128]{0:T(128)}, u32[]{:S(2)}) copy-start(f32[128]{0:T(128)} %param.15) | copy-start | bytes 1540
  397.6 38.3 %copy-start.2 = (f32[128,256]{1,0:T(8,128)S(1)}, f32[128,256]{1,0:T(8,128)}, u32[]{:S(2)}) copy-start(f32[128,256]{1,0:T(8,128)} %reduce-scatter.14.cloned.1.call-done) | copy-start | bytes 393220
  398.6 5.3 %collective-permute-start = (f32[128,256]{1,0:T(8,128)S(1)}, f32[128,256]{1,0:T(8,128)S(1)}, u32[]{:S(2)}, u32[]{:S(2)}) collective-permute-start(f32[128,256]{1,0:T(8,128)S(1)} %maximum_divide_fusion), channel_id=1, source_target_pairs={{0,4},{4,8},{8,12},{12,16},{16,20},{20,24},{24,28},{28,0},{1,5},{5... | collective-permute-start | bytes 393224 | tf_op jit(solution)/shard_map/ppermute | solution.py:75
  404.0 5.3 %collective-permute-start.1 = (f32[128,256]{1,0:T(8,128)S(1)}, f32[128,256]{1,0:T(8,128)S(1)}, u32[]{:S(2)}, u32[]{:S(2)}) collective-permute-start(f32[128,256]{1,0:T(8,128)S(1)} %collective-permute-done), channel_id=1, source_target_pairs={{0,4},{4,8},{8,12},{12,16},{16,20},{20,24},{24,28},{28,0},{1,5},{5... | collective-permute-start | bytes 393224 | tf_op jit(solution)/shard_map/ppermute | solution.py:75
  409.3 5.3 %collective-permute-start.2 = (f32[128,256]{1,0:T(8,128)S(1)}, f32[128,256]{1,0:T(8,128)S(1)}, u32[]{:S(2)}, u32[]{:S(2)}) collective-permute-start(f32[128,256]{1,0:T(8,128)S(1)} %collective-permute-done.1), channel_id=1, source_target_pairs={{0,4},{4,8},{8,12},{12,16},{16,20},{20,24},{24,28},{28,0},{1,5},{5... | collective-permute-start | bytes 393224 | tf_op jit(solution)/shard_map/ppermute | solution.py:75
  414.6 5.3 %collective-permute-start.3 = (f32[128,256]{1,0:T(8,128)S(1)}, f32[128,256]{1,0:T(8,128)S(1)}, u32[]{:S(2)}, u32[]{:S(2)}) collective-permute-start(f32[128,256]{1,0:T(8,128)S(1)} %collective-permute-done.2), channel_id=1, source_target_pairs={{0,4},{4,8},{8,12},{12,16},{16,20},{20,24},{24,28},{28,0},{1,5},{5... | collective-permute-start | bytes 393224 | tf_op jit(solution)/shard_map/ppermute | solution.py:75
  419.9 5.3 %collective-permute-start.4 = (f32[128,256]{1,0:T(8,128)S(1)}, f32[128,256]{1,0:T(8,128)S(1)}, u32[]{:S(2)}, u32[]{:S(2)}) collective-permute-start(f32[128,256]{1,0:T(8,128)S(1)} %collective-permute-done.3), channel_id=1, source_target_pairs={{0,4},{4,8},{8,12},{12,16},{16,20},{20,24},{24,28},{28,0},{1,5},{5... | collective-permute-start | bytes 393224 | tf_op jit(solution)/shard_map/ppermute | solution.py:75
  425.1 5.3 %collective-permute-start.5 = (f32[128,256]{1,0:T(8,128)S(1)}, f32[128,256]{1,0:T(8,128)S(1)}, u32[]{:S(2)}, u32[]{:S(2)}) collective-permute-start(f32[128,256]{1,0:T(8,128)S(1)} %collective-permute-done.4), channel_id=1, source_target_pairs={{0,4},{4,8},{8,12},{12,16},{16,20},{20,24},{24,28},{28,0},{1,5},{5... | collective-permute-start | bytes 393224 | tf_op jit(solution)/shard_map/ppermute | solution.py:75
  430.4 5.3 %collective-permute-start.6 = (f32[128,256]{1,0:T(8,128)S(1)}, f32[128,256]{1,0:T(8,128)S(1)}, u32[]{:S(2)}, u32[]{:S(2)}) collective-permute-start(f32[128,256]{1,0:T(8,128)S(1)} %collective-permute-done.5), channel_id=1, source_target_pairs={{0,4},{4,8},{8,12},{12,16},{16,20},{20,24},{24,28},{28,0},{1,5},{5... | collective-permute-start | bytes 393224 | tf_op jit(solution)/shard_map/ppermute | solution.py:75
  439.3 2.4 copy-start.1
Sparse Core Ops, SparseCore 0:
  10.6 39.4 all-gather.4
  52.0 36.7 all-gather.6
  90.7 36.7 all-gather.8
  129.2 36.7 all-gather.10
  168.1 43.8 reduce-scatter.5
  214.2 43.1 reduce-scatter.7
  259.7 43.1 reduce-scatter.9
  305.9 43.1 reduce-scatter.11
  362.2 35.3 reduce-scatter.13
